TPU v7x, 32 devices: a whole 2x2x4 slice. The times are simulated.
32 devices in a mesh: dp: 8 (over z, y), row: 2 (over core), col: 2 (over x).
Axes of the slice: x: 2, y: 2, z: 4, core: 2. Of those that a mesh axis runs over, the one named last changes fastest.
Arguments:
- tokens: bfloat16 [8192, 2048], P(('dp', 'row', 'col')), may hold values from -6 to 6
- segments: int32 [8, 1024], P('dp'), may hold values from 0 to 7, never falling along the last dimension, each value on 1 to 512 neighbouring positions
- attn_gain: float32 [2048], replicated, may hold values from 0.5 to 1.5
- w_query: bfloat16 [2048, 2048], P(None, ('row', 'col')), may hold values from -0.125 to 0.125
- w_key: bfloat16 [2048, 256], P(None, ('row', 'col')), may hold values from -0.125 to 0.125
- w_value: bfloat16 [2048, 256], P(None, ('row', 'col')), may hold values from -0.125 to 0.125
- w_out: bfloat16 [2048, 2048], P(('row', 'col')), may hold values from -0.75 to 0.75
- ffn_gain: float32 [2048], replicated, may hold values from 0.5 to 1.5
- w_gate: bfloat16 [2048, 5632], P(None, ('row', 'col')), may hold values from -0.125 to 0.125
- w_up: bfloat16 [2048, 5632], P(None, ('row', 'col')), may hold values from -0.125 to 0.125
- w_down: bfloat16 [5632, 2048], P(('row', 'col')), may hold values from -0.078125 to 0.078125
- out_cotangent: bfloat16 [8192, 2048], P(('dp', 'row', 'col')), may hold values from -6 to 6
Outputs:
- mixed: bfloat16 [8192, 2048], P(('dp', 'row', 'col'))
- input_grad: float32 [8192, 2048], P(('dp', 'row', 'col'))
- attn_gain_grad: float32 [2048], replicated
- query_grad: float32 [2048, 2048], P('dp', ('row', 'col'))
- key_grad: float32 [2048, 256], P('dp', ('row', 'col'))
- value_grad: float32 [2048, 256], P('dp', ('row', 'col'))
- out_proj_grad: float32 [2048, 2048], P(('row', 'col'), 'dp')
- ffn_gain_grad: float32 [2048], replicated
- gate_grad: float32 [2048, 5632], P('dp', ('row', 'col'))
- up_grad: float32 [2048, 5632], P('dp', ('row', 'col'))
- down_grad: float32 [5632, 2048], P(('row', 'col'), 'dp')
Inputs may be any that keep to these rules, and one draw needn't show every extreme that they name: `segments`: within each sequence document numbers never fall; each document has 1 to 512 tokens, and one has exactly 512.
All inputs are finite; a program needn't handle non-finite values.
Results may differ from a plain program's by a relative error of at most 0.02.
Values may be sent and summed in bfloat16 or wider, within the bound.
No kernel may reach another device: no remote copies, remote signals or barrier semaphores. Data moves between devices by JAX's collectives and lax.ppermute only.
A program may use at most 256 MiB of HBM per device.

v0:
```python
import jax
import jax.numpy as jnp
from jax import lax
from jax.sharding import PartitionSpec as P

HD = 64


EPSILON = 1e-05
MASKED_SCORE = -1e30


def positions(segment_ids):
    indices = jnp.arange(segment_ids.shape[-1], dtype=jnp.int32)
    previous = jnp.concatenate([segment_ids[..., :1] - 1, segment_ids[..., :-1]], axis=-1)
    starts = jnp.where(segment_ids != previous, indices, 0)
    return indices - lax.cummax(starts, axis=segment_ids.ndim - 1)


def rotate(values, position, direction):
    half_dim = values.shape[-1] // 2
    exponent = jnp.arange(half_dim, dtype=jnp.float32) * (-2.0 / values.shape[-1])
    angles = position.astype(jnp.float32)[:, None] * (10000.0**exponent)[None, :]
    cosine = jnp.concatenate([jnp.cos(angles), jnp.cos(angles)], axis=-1)[:, None, :]
    sine = jnp.concatenate([jnp.sin(angles), jnp.sin(angles)], axis=-1)[:, None, :]
    first_half = values[..., :half_dim]
    second_half = values[..., half_dim:]
    turned = jnp.concatenate([-second_half, first_half], axis=-1)
    return values * cosine + turned * (direction * sine)


def dot_last(left, right):
    return lax.dot_general(
        left, right, (((1,), (1,)), ((), ())), preferred_element_type=jnp.float32
    )


def dot_first(left, right):
    return lax.dot_general(
        left, right, (((0,), (0,)), ((), ())), preferred_element_type=jnp.float32
    )


def norm_back(grad_normed, unit_rows, inverse, gain):
    scaled = grad_normed * gain
    inner = jnp.mean(scaled * unit_rows, axis=-1, keepdims=True)
    return (inverse * (scaled - unit_rows * inner), jnp.sum(grad_normed * unit_rows, axis=0))


def block_scores(query_block, key_seq, seg_query, seg_keys, first_row):
    raw = jnp.einsum(
        "qhgd,khd->hgqk", query_block, key_seq, preferred_element_type=jnp.float32
    ) * HD ** (-0.5)
    query_at = first_row + jnp.arange(query_block.shape[0])
    key_at = jnp.arange(key_seq.shape[0])
    allowed = (seg_query[:, None] == seg_keys[None, :]) & (key_at[None, :] <= query_at[:, None])
    return (jnp.where(allowed, raw, MASKED_SCORE), allowed)


def local(
    tokens,
    segments,
    attn_gain,
    w_query,
    w_key,
    w_value,
    w_out,
    ffn_gain,
    w_gate,
    w_up,
    w_down,
    out_cotangent,
):
    inputs = tokens.astype(jnp.float32)
    seq_count, length = segments.shape
    all_rows = seq_count * length
    query_width = w_query.shape[1]
    kv_width = w_key.shape[1]
    kv_heads = kv_width // HD
    ffn_width = w_gate.shape[1]
    block_rows = min(512, length)
    blocks = length // block_rows
    block_total = seq_count * blocks
    position = positions(segments).reshape(all_rows)
    qkv_weight = jnp.concatenate([w_query, w_key, w_value], axis=1)
    inverse_one = lax.rsqrt(jnp.mean(inputs * inputs, axis=-1, keepdims=True) + EPSILON)
    unit_one = inputs * inverse_one
    normed_one = (unit_one * attn_gain).astype(jnp.bfloat16)
    gathered_one = lax.all_gather(normed_one, ("row", "col"), axis=0, tiled=True)
    projected = jnp.dot(gathered_one, qkv_weight, preferred_element_type=jnp.float32)
    queries = rotate(projected[:, :query_width].reshape(all_rows, -1, HD), position, 1.0).astype(
        jnp.bfloat16
    )
    queries = queries.reshape(seq_count, length, kv_heads, -1, HD)
    key_rows = rotate(
        projected[:, query_width : query_width + kv_width].reshape(all_rows, kv_heads, HD),
        position,
        1.0,
    )
    key_rows = key_rows.astype(jnp.bfloat16).reshape(seq_count, length, kv_heads, HD)
    value_rows = (
        projected[:, query_width + kv_width :]
        .astype(jnp.bfloat16)
        .reshape(seq_count, length, kv_heads, HD)
    )

    def block_parts(number):
        sequence = number // blocks
        first_row = number % blocks * block_rows
        query_seq = lax.dynamic_index_in_dim(queries, sequence, 0, keepdims=False)
        query_block = lax.dynamic_slice_in_dim(query_seq, first_row, block_rows, 0)
        key_seq = lax.dynamic_index_in_dim(key_rows, sequence, 0, keepdims=False)
        value_seq = lax.dynamic_index_in_dim(value_rows, sequence, 0, keepdims=False)
        seg_keys = lax.dynamic_index_in_dim(segments, sequence, 0, keepdims=False)
        seg_query = lax.dynamic_slice_in_dim(seg_keys, first_row, block_rows, 0)
        masked, allowed = block_scores(query_block, key_seq, seg_query, seg_keys, first_row)
        return (query_block, key_seq, value_seq, masked, allowed, sequence, first_row)

    def attend_block(number):
        query_block, key_seq, value_seq, masked, allowed, sequence, first_row = block_parts(number)
        largest = jnp.max(masked, axis=-1, keepdims=True)
        shifted = jnp.exp(masked - largest)
        row_total = jnp.sum(shifted, axis=-1, keepdims=True)
        weights = (shifted / row_total).astype(jnp.bfloat16)
        mixture = jnp.einsum(
            "hgqk,khd->qhgd", weights, value_seq, preferred_element_type=jnp.float32
        )
        return (
            mixture.reshape(block_rows, -1).astype(jnp.bfloat16),
            (largest + jnp.log(row_total))[..., 0],
        )

    attn_mixed, log_sums = lax.map(attend_block, jnp.arange(block_total))
    attn_mixed = attn_mixed.reshape(all_rows, query_width)
    middle = inputs + lax.psum_scatter(
        jnp.dot(attn_mixed, w_out, preferred_element_type=jnp.float32).astype(jnp.bfloat16),
        ("row", "col"),
        scatter_dimension=0,
        tiled=True,
    ).astype(jnp.float32)
    inverse_two = lax.rsqrt(jnp.mean(middle * middle, axis=-1, keepdims=True) + EPSILON)
    unit_two = middle * inverse_two
    normed_two = (unit_two * ffn_gain).astype(jnp.bfloat16)
    gathered_two = lax.all_gather(normed_two, ("row", "col"), axis=0, tiled=True)
    gate_pre = jnp.dot(gathered_two, w_gate, preferred_element_type=jnp.float32)
    up_pre = jnp.dot(gathered_two, w_up, preferred_element_type=jnp.float32)
    sigmoid_gate = jax.nn.sigmoid(gate_pre)
    hidden = (gate_pre * sigmoid_gate * up_pre).astype(jnp.bfloat16)
    output = middle + lax.psum_scatter(
        jnp.dot(hidden, w_down, preferred_element_type=jnp.float32).astype(jnp.bfloat16),
        ("row", "col"),
        scatter_dimension=0,
        tiled=True,
    ).astype(jnp.float32)
    mixed_out = output.astype(jnp.bfloat16)
    grad_out = out_cotangent.astype(jnp.float32)
    grad_rows = lax.all_gather(out_cotangent, ("row", "col"), axis=0, tiled=True)
    grad_hidden = dot_last(grad_rows, w_down)
    slope = sigmoid_gate + gate_pre * sigmoid_gate * (1.0 - sigmoid_gate)
    grad_gate = (grad_hidden * up_pre * slope).astype(jnp.bfloat16)
    grad_up = (grad_hidden * gate_pre * sigmoid_gate).astype(jnp.bfloat16)
    grad_normed_two = lax.psum_scatter(
        (dot_last(grad_gate, w_gate) + dot_last(grad_up, w_up)).astype(jnp.bfloat16),
        ("row", "col"),
        scatter_dimension=0,
        tiled=True,
    ).astype(jnp.float32)
    ffn_terms = jnp.concatenate(
        [
            dot_first(gathered_two, grad_gate),
            dot_first(gathered_two, grad_up),
            dot_first(grad_rows, hidden),
        ],
        axis=1,
    )
    grad_middle_norm, gain_two_grad = norm_back(grad_normed_two, unit_two, inverse_two, ffn_gain)
    grad_middle = grad_out + grad_middle_norm
    grad_attn_rows = lax.all_gather(
        grad_middle.astype(jnp.bfloat16), ("row", "col"), axis=0, tiled=True
    )
    grad_mixed = (
        dot_last(grad_attn_rows, w_out)
        .astype(jnp.bfloat16)
        .reshape(seq_count, length, kv_heads, -1, HD)
    )

    def attend_back(number):
        query_block, key_seq, value_seq, masked, allowed, sequence, first_row = block_parts(number)
        grad_seq = lax.dynamic_index_in_dim(grad_mixed, sequence, 0, keepdims=False)
        grad_block = lax.dynamic_slice_in_dim(grad_seq, first_row, block_rows, 0)
        log_block = lax.dynamic_index_in_dim(log_sums, number, 0, keepdims=False)
        probs = jnp.where(allowed, jnp.exp(masked - log_block[..., None]), 0.0)
        grad_probs = jnp.einsum(
            "qhgd,khd->hgqk", grad_block, value_seq, preferred_element_type=jnp.float32
        )
        inner = jnp.sum(probs * grad_probs, axis=-1, keepdims=True)
        grad_scores = (probs * (grad_probs - inner)).astype(jnp.bfloat16)
        factor = HD ** (-0.5)
        grad_query = (
            jnp.einsum("hgqk,khd->qhgd", grad_scores, key_seq, preferred_element_type=jnp.float32)
            * factor
        )
        grad_key = (
            jnp.einsum(
                "hgqk,qhgd->khd", grad_scores, query_block, preferred_element_type=jnp.float32
            )
            * factor
        )
        grad_value = jnp.einsum(
            "hgqk,qhgd->khd",
            probs.astype(jnp.bfloat16),
            grad_block,
            preferred_element_type=jnp.float32,
        )
        return (grad_query, grad_key, grad_value)

    grad_query, grad_key, grad_value = lax.map(attend_back, jnp.arange(block_total))
    grad_query = (
        rotate(grad_query.reshape(all_rows, -1, HD), position, -1.0)
        .reshape(all_rows, query_width)
        .astype(jnp.bfloat16)
    )
    grad_key = jnp.sum(grad_key.reshape(seq_count, blocks, length, kv_heads, HD), axis=1).reshape(
        all_rows, kv_heads, HD
    )
    grad_key = rotate(grad_key, position, -1.0).reshape(all_rows, kv_width).astype(jnp.bfloat16)
    grad_value = (
        jnp.sum(grad_value.reshape(seq_count, blocks, length, kv_width), axis=1)
        .reshape(all_rows, kv_width)
        .astype(jnp.bfloat16)
    )
    grad_qkv = jnp.concatenate([grad_query, grad_key, grad_value], axis=1)
    grad_normed_one = lax.psum_scatter(
        dot_last(grad_qkv, qkv_weight).astype(jnp.bfloat16),
        ("row", "col"),
        scatter_dimension=0,
        tiled=True,
    ).astype(jnp.float32)
    attn_terms = jnp.concatenate(
        [dot_first(gathered_one, grad_qkv), dot_first(grad_attn_rows, attn_mixed)], axis=1
    )
    attn_sums, ffn_sums = (
        lax.psum_scatter(
            attn_terms.astype(jnp.bfloat16), "dp", scatter_dimension=0, tiled=True
        ).astype(jnp.float32),
        lax.psum_scatter(
            ffn_terms.astype(jnp.bfloat16), "dp", scatter_dimension=0, tiled=True
        ).astype(jnp.float32),
    )
    grad_input_norm, gain_one_grad = norm_back(grad_normed_one, unit_one, inverse_one, attn_gain)
    input_grad = grad_middle + grad_input_norm
    gain_one_total, gain_two_total = lax.psum((gain_one_grad, gain_two_grad), ("dp", "row", "col"))
    key_end = query_width + kv_width
    value_end = key_end + kv_width
    return (
        mixed_out,
        input_grad,
        gain_one_total,
        attn_sums[:, :query_width],
        attn_sums[:, query_width:key_end],
        attn_sums[:, key_end:value_end],
        attn_sums[:, value_end:].T,
        gain_two_total,
        ffn_sums[:, :ffn_width],
        ffn_sums[:, ffn_width : 2 * ffn_width],
        ffn_sums[:, 2 * ffn_width :].T,
    )


def solution(mesh):
    placed = (
        P(("dp", "row", "col"), None),
        P("dp", None),
        P(),
        P(None, ("row", "col")),
        P(None, ("row", "col")),
        P(None, ("row", "col")),
        P(("row", "col"), None),
        P(),
        P(None, ("row", "col")),
        P(None, ("row", "col")),
        P(("row", "col"), None),
        P(("dp", "row", "col"), None),
    )
    return jax.shard_map(
        local,
        mesh=mesh,
        in_specs=placed,
        out_specs=(
            P(("dp", "row", "col"), None),
            P(("dp", "row", "col"), None),
            P(),
            P("dp", ("row", "col")),
            P("dp", ("row", "col")),
            P("dp", ("row", "col")),
            P(("row", "col"), "dp"),
            P(),
            P("dp", ("row", "col")),
            P("dp", ("row", "col")),
            P(("row", "col"), "dp"),
        ),
        check_vma=False,
    )
```

profile of v0, /device:TPU:0, one launch (start us, length us, event | category | flops | bytes accessed | tf_op | source)
XLA Modules:
  0.0 995.0 jit_solution(9201300982560241220)
XLA Ops:
  14.7 34.1 %all-gather.5.cloned.1.call-done = bf16[1024,2048]{1,0:T(8,128)(2,1)} async-done(((bf16[256,2048]{1,0:T(8,128)(2,1)}), bf16[1024,2048]{1,0:T(8,128)(2,1)}) %all-gather.5.cloned.1.call-update) | async-done | bytes 4194320 | tf_op jit(solution)/shard_map/all_gather | solution.py:89
  57.5 37.2 %while.30 = (s32[]{:T(128)}, bf16[2,512,512]{2,1,0:T(8,128)(2,1)}, f32[2,1,8,512]{3,2,1,0:T(8,128)}, s32[2]{0:T(128)S(1)}, s32[1,1024]{1,0:T(1,128)S(1)}, /*inde...) while((s32[]{:T(128)}, bf16[2,512,512]{2,1,0:T(8,128)(2,1)}, ...), condition=%wide.region_6.7_spmd, body=%wide.region_3.6_spmd.sunk | while | flops 1125904896 | bytes 55982400 | solution.py:133
  100.3 44.6 %reduce-scatter.7.cloned.1.call-done = bf16[256,2048]{1,0:T(8,128)(2,1)} async-done(((bf16[1024,2048]{1,0:T(8,128)(2,1)}), bf16[256,2048]{1,0:T(8,128)(2,1)}) %reduce-scatter.7.cloned.1.call-update) | async-done | bytes 1048592 | tf_op jit(solution)/shard_map/reduce_scatter | solution.py:135
  149.8 34.0 %all-gather.7.cloned.1.call-done = bf16[1024,2048]{1,0:T(8,128)(2,1)} async-done(((bf16[256,2048]{1,0:T(8,128)(2,1)}), bf16[1024,2048]{1,0:T(8,128)(2,1)}) %all-gather.7.cloned.1.call-update) | async-done | bytes 4194320 | tf_op jit(solution)/shard_map/all_gather | solution.py:144
  183.9 12.1 %fusion.95 = f32[1024,1408]{1,0:T(8,128)} fusion(bf16[1024,2048]{1,0:T(8,128)(2,1)} %all-gather.7.cloned.1.call-done, bf16[2048,1408]{1,0:T(8,128)(2,1)} %param.25), kind=kOutput, calls=%fused_computation.164 | convolution fusion | flops 5905580032 | bytes 15728640 | tf_op jit(solution)/shard_map/dot_general | solution.py:146
  196.0 10.3 %fusion.94 = f32[1024,1408]{1,0:T(8,128)} fusion(bf16[1024,2048]{1,0:T(8,128)(2,1)S(1)} %copy-done.40, bf16[2048,1408]{1,0:T(8,128)(2,1)} %param.24), kind=kOutput, calls=%fused_computation.163 | convolution fusion | flops 5905580032 | bytes 15728640 | tf_op jit(solution)/shard_map/dot_general | solution.py:145
  206.3 13.6 %all-gather.9.cloned.1.call-done = bf16[1024,2048]{1,0:T(8,128)(2,1)} async-done(((bf16[256,2048]{1,0:T(8,128)(2,1)}), bf16[1024,2048]{1,0:T(8,128)(2,1)}) %all-gather.9.cloned.1.call-update) | async-done | bytes 4194320 | tf_op jit(solution)/shard_map/all_gather | solution.py:157
  219.9 15.4 %multiply_convert_fusion = (bf16[1024,1408]{1,0:T(8,128)(2,1)S(1)}, bf16[1024,1408]{1,0:T(8,128)(2,1)S(1)}, bf16[1024,1408]{1,0:T(8,128)(2,1)}) fusion(f32[1024,1408]{1,0:T(8,128)} %fusion.94, f32[1024,1408]{1,0:T(8,128)} %fusion.95, bf16[1024,2048]{1,0:T(8,128)(2,1)} %all-gather.9.cloned.1.call-done, bf16[1408,2048]{1,0:T(8,128)(2,1)} %param.26), kind=kOutput, calls=%fused_computation.70 | convolution fusion | flops 5927206912 | bytes 30146560 | tf_op jit(solution)/shard_map/dot_general | solution.py:33
  235.3 10.8 %fusion.96 = f32[1024,2048]{1,0:T(8,128)S(1)} fusion(bf16[1024,1408]{1,0:T(8,128)(2,1)S(1)} %get-tuple-element.330, bf16[2048,1408]{1,0:T(8,128)(2,1)} %param.24), kind=kOutput, calls=%fused_computation.165 | convolution fusion | flops 5905580032 | bytes 17039360 | tf_op jit(solution)/shard_map/dot_general | solution.py:33
  246.2 11.6 %add_convert_fusion = bf16[1024,2048]{1,0:T(8,128)(2,1)} fusion(f32[1024,2048]{1,0:T(8,128)S(1)} %fusion.96, bf16[1024,1408]{1,0:T(8,128)(2,1)S(1)} %get-tuple-element.329, bf16[2048,1408]{1,0:T(8,128)(2,1)} %param.25), kind=kOutput, calls=%fused_computation.65 | convolution fusion | flops 5909774336 | bytes 21233664 | tf_op jit(solution)/shard_map/dot_general | solution.py:33
  257.8 44.6 %reduce-scatter.11.cloned.1.call-done = bf16[256,2048]{1,0:T(8,128)(2,1)} async-done(((bf16[1024,2048]{1,0:T(8,128)(2,1)}), bf16[256,2048]{1,0:T(8,128)(2,1)}) %reduce-scatter.11.cloned.1.call-update) | async-done | bytes 1048592 | tf_op jit(solution)/shard_map/reduce_scatter | solution.py:162
  307.9 34.6 %all-gather.11.cloned.1.call-done = bf16[1024,2048]{1,0:T(8,128)(2,1)} async-done(((bf16[256,2048]{1,0:T(8,128)(2,1)}), bf16[1024,2048]{1,0:T(8,128)(2,1)}) %all-gather.11.cloned.1.call-update) | async-done | bytes 4194320 | tf_op jit(solution)/shard_map/all_gather | solution.py:178
  347.0 127.6 %while.31 = (s32[]{:T(128)}, f32[2,512,1,8,64]{1,0,4,3,2:T(2,128)}, f32[2,1024,1,64]{1,3,2,0:T(8,128)}, f32[2,1024,1,64]{1,3,2,0:T(8,128)}, s32[2]{0:T(128)S(1)}...) while((s32[]{:T(128)}, f32[2,512,1,8,64]{1,0,4,3,2:T(2,128)}, ...), condition=%wide.region_14.15_spmd, body=%wide.region_12.14_spmd.sunk | while | flops 2728194560 | bytes 143620592 | solution.py:217
  357.0 12.1 %fusion.162 = (f32[8,512]{1,0:T(8,128)}, f32[1,8,512,1024]{3,2,1,0:T(8,128)}) fusion(f32[512,8,1024]{2,0,1:T(8,128)S(1)} %fusion.160, f32[8,512]{1,0:T(8,128)} %dynamic-slice_bitcast_fusion.2, bf16[1,1024,1,64]{1,3,2,0:T(8,128)(2,1)} %get-tuple-element.555, bf16[1,1024,1,8,64]{1,4,3,2,0:T(8,128)(2,1)} %get-tuple-element.554, s32[]{:T(128)S(6)} %select_n.117, ...), kind=kOutput, calls=%fused_computation.28.clone.1 | convolution fusion | flops 562032640 | bytes 34766852 | tf_op jit(solution)/shard_map/while/body/eval_jaxpr/qhgd,khd->hgqk/dot_general | solution.py:51
  376.0 7.4 fusion.166
  391.2 19.6 %dynamic_update_slice.47 = f32[2,512,1,8,64]{1,0,4,3,2:T(2,128)} dynamic-update-slice(f32[2,512,1,8,64]{1,0,4,3,2:T(2,128)} %get-tuple-element.533, f32[1,512,1,8,64]{1,0,4,3,2:T(1,128)S(1)} %copy.55, s32[]{:T(128)S(6)} %copy.74, s32[]{:T(128)} %constant.198.clone.1..sunk.1, s32[]{:T(128)} %constant.198.clone.1..sunk.1, s32[]{:T(128)} %constant.198.clone.1..sunk.1, s32[]{:T(128)} %constant.198.clone.1..sunk.1) | dynamic-update-slice | bytes 2097156 | tf_op jit(solution)/shard_map/while/body/jit(dynamic_update_index_in_dim)/dynamic_update_slice | solution.py:217
  420.6 12.1 %fusion.162 = (f32[8,512]{1,0:T(8,128)}, f32[1,8,512,1024]{3,2,1,0:T(8,128)}) fusion(f32[512,8,1024]{2,0,1:T(8,128)S(1)} %fusion.160, f32[8,512]{1,0:T(8,128)} %dynamic-slice_bitcast_fusion.2, bf16[1,1024,1,64]{1,3,2,0:T(8,128)(2,1)} %get-tuple-element.555, bf16[1,1024,1,8,64]{1,4,3,2,0:T(8,128)(2,1)} %get-tuple-element.554, s32[]{:T(128)S(6)} %select_n.117, ...), kind=kOutput, calls=%fused_computation.28.clone.1 | convolution fusion | flops 562032640 | bytes 34766852 | tf_op jit(solution)/shard_map/while/body/eval_jaxpr/qhgd,khd->hgqk/dot_general | solution.py:51
  454.8 19.6 %dynamic_update_slice.47 = f32[2,512,1,8,64]{1,0,4,3,2:T(2,128)} dynamic-update-slice(f32[2,512,1,8,64]{1,0,4,3,2:T(2,128)} %get-tuple-element.533, f32[1,512,1,8,64]{1,0,4,3,2:T(1,128)S(1)} %copy.55, s32[]{:T(128)S(6)} %copy.74, s32[]{:T(128)} %constant.198.clone.1..sunk.1, s32[]{:T(128)} %constant.198.clone.1..sunk.1, s32[]{:T(128)} %constant.198.clone.1..sunk.1, s32[]{:T(128)} %constant.198.clone.1..sunk.1) | dynamic-update-slice | bytes 2097156 | tf_op jit(solution)/shard_map/while/body/jit(dynamic_update_index_in_dim)/dynamic_update_slice | solution.py:217
  491.6 10.9 %convolution_convert_fusion.4 = bf16[1024,2048]{1,0:T(8,128)(2,1)} fusion(bf16[1024,1408]{1,0:T(8,128)(2,1)} %get-tuple-element.331, bf16[1408,2048]{1,0:T(8,128)(2,1)} %param.26), kind=kOutput, calls=%fused_computation.76 | convolution fusion | flops 5907677184 | bytes 12845056 | tf_op jit(solution)/shard_map/dot_general | solution.py:150
  515.2 9.5 convolution_convert_fusion.1
  537.9 7.7 pad_maximum_fusion
  549.7 39.7 %all-reduce = (f32[2048]{0:T(1024)}, f32[2048]{0:T(1024)}) all-reduce(f32[2048]{0:T(1024)S(1)} %get-tuple-element.283, f32[2048]{0:T(1024)S(1)} %copy-done.32), channel_id=1, replica_groups=mesh['dp'=8,'row'=2,'col'=2] {'dp','row','col'}, use_global_device_ids=true, to_apply=%region_20.21 | all-reduce | flops 4096 | bytes 32768 | tf_op jit(solution)/shard_map/psum | solution.py:252
  594.6 88.4 %reduce-scatter.15.cloned.1.call-done = bf16[256,1152]{0,1:T(8,128)(2,1)} async-done(((bf16[2048,1152]{0,1:T(8,128)(2,1)}), bf16[256,1152]{0,1:T(8,128)(2,1)}) %reduce-scatter.15.cloned.1.call-update) | async-done | bytes 589840 | tf_op jit(solution)/shard_map/reduce_scatter | solution.py:243
  688.5 291.6 %reduce-scatter.17.cloned.1.call-done = bf16[256,4224]{0,1:T(8,128)(2,1)} async-done(((bf16[2048,4224]{0,1:T(8,128)(2,1)}), bf16[256,4224]{0,1:T(8,128)(2,1)}) %reduce-scatter.17.cloned.1.call-update) | async-done | bytes 2162704 | tf_op jit(solution)/shard_map/reduce_scatter | solution.py:246
  (235 shorter events, 183.5 us)
Async XLA Ops:
  7.2 87.5 %copy-start = (bf16[512,2048]{1,0:T(8,128)(2,1)S(1)}, bf16[512,2048]{1,0:T(8,128)(2,1)}, u32[]{:S(2)}) copy-start(bf16[512,2048]{1,0:T(8,128)(2,1)} %param.22) | copy-start | bytes 6291460
  7.2 41.6 %all-gather.5.cloned.1.call-start = ((), (), s32[]{:S(2)}) async-start(), calls=%async_computation.6 | async-start | bytes 5242880 | tf_op jit(solution)/shard_map/all_gather | solution.py:89
  11.5 133.4 %reduce-scatter.7.cloned.1.call-start = ((), (), s32[]{:S(2)}) async-start(), calls=%async_computation.7 | async-start | bytes 5242880 | tf_op jit(solution)/shard_map/reduce_scatter | solution.py:135
  13.8 40.9 %copy-start.19 = (bf16[2048,64]{1,0:T(8,128)(2,1)}, bf16[2048,64]{1,0:T(8,128)(2,1)S(1)}, u32[]{:S(2)}) copy-start(bf16[2048,64]{1,0:T(8,128)(2,1)S(1)} %copy.31) | copy-start | bytes 786436
  14.0 40.6 %copy-start.21 = (bf16[2048,64]{1,0:T(8,128)(2,1)}, bf16[2048,64]{1,0:T(8,128)(2,1)S(1)}, u32[]{:S(2)}) copy-start(bf16[2048,64]{1,0:T(8,128)(2,1)S(1)} %copy.32) | copy-start | bytes 786436
  14.7 40.5 %copy-start.15 = (f32[1024,32]{0,1:T(8,128)}, f32[1024,32]{0,1:T(8,128)S(1)}, u32[]{:S(2)}) copy-start(f32[1024,32]{0,1:T(8,128)S(1)} %get-tuple-element.351) | copy-start | bytes 393220
  14.7 40.5 %copy-start.17 = (f32[1024,32]{0,1:T(8,128)}, f32[1024,32]{0,1:T(8,128)S(1)}, u32[]{:S(2)}) copy-start(f32[1024,32]{0,1:T(8,128)S(1)} %get-tuple-element.352) | copy-start | bytes 393220
  100.2 44.7 %copy-start.2 = (bf16[256,2048]{1,0:T(8,128)(2,1)S(1)}, bf16[256,2048]{1,0:T(8,128)(2,1)}, u32[]{:S(2)}) copy-start(bf16[256,2048]{1,0:T(8,128)(2,1)} %param.16) | copy-start | bytes 3145732
  100.2 46.3 %copy-start.29 = (f32[2048]{0:T(1024)S(1)}, f32[2048]{0:T(1024)}, u32[]{:S(2)}) copy-start(f32[2048]{0:T(1024)} %param.23) | copy-start | bytes 24580
  100.3 83.6 %all-gather.7.cloned.1.call-start = ((), (), s32[]{:S(2)}) async-start(), calls=%async_computation.8 | async-start | bytes 5242880 | tf_op jit(solution)/shard_map/all_gather | solution.py:144
  146.6 159.1 %copy-start.33 = (f32[256]{0:T(256)}, f32[256]{0:T(256)S(1)}, u32[]{:S(2)}) copy-start(f32[256]{0:T(256)S(1)} %add_rsqrt_fusion) | copy-start | bytes 3076
  149.2 70.7 %all-gather.9.cloned.1.call-start = ((), (), s32[]{:S(2)}) async-start(), calls=%async_computation.10 | async-start | bytes 5242880 | tf_op jit(solution)/shard_map/all_gather | solution.py:157
  149.8 152.7 %reduce-scatter.11.cloned.1.call-start = ((), (), s32[]{:S(2)}) async-start(), calls=%async_computation.11 | async-start | bytes 5242880 | tf_op jit(solution)/shard_map/reduce_scatter | solution.py:162
  183.9 12.1 %copy-start.40 = (bf16[1024,2048]{1,0:T(8,128)(2,1)S(1)}, bf16[1024,2048]{1,0:T(8,128)(2,1)}, u32[]{:S(2)}) copy-start(bf16[1024,2048]{1,0:T(8,128)(2,1)} %all-gather.7.cloned.1.call-done) | copy-start | bytes 12582916
  257.8 84.7 %all-gather.11.cloned.1.call-start = ((), (), s32[]{:S(2)}) async-start(), calls=%async_computation.12 | async-start | bytes 5242880 | tf_op jit(solution)/shard_map/all_gather | solution.py:178
  307.8 237.9 %reduce-scatter.13.cloned.1.call-start = ((), (), s32[]{:S(2)}) async-start(), calls=%async_computation.13 | async-start | bytes 5242880 | tf_op jit(solution)/shard_map/reduce_scatter | solution.py:233
  491.5 97.9 %reduce-scatter.9.cloned.1.call-start = ((), (), s32[]{:S(2)}) async-start(), calls=%async_computation.9 | async-start | bytes 5242880 | tf_op jit(solution)/shard_map/reduce_scatter | solution.py:149
  502.5 180.5 %reduce-scatter.15.cloned.1.call-start = ((), (), s32[]{:S(2)}) async-start(), calls=%async_computation.14 | async-start | bytes 5308416 | tf_op jit(solution)/shard_map/reduce_scatter | solution.py:243
  515.2 464.9 %reduce-scatter.17.cloned.1.call-start = ((), (), s32[]{:S(2)}) async-start(), calls=%async_computation.15 | async-start | bytes 19464192 | tf_op jit(solution)/shard_map/reduce_scatter | solution.py:246
  545.6 43.8 %copy-start.5 = (bf16[256,2048]{1,0:T(8,128)(2,1)S(1)}, bf16[256,2048]{1,0:T(8,128)(2,1)}, u32[]{:S(2)}) copy-start(bf16[256,2048]{1,0:T(8,128)(2,1)} %reduce-scatter.7.cloned.1.call-done) | copy-start | bytes 3145732
  545.6 43.8 %copy-start.7 = (bf16[256,2048]{1,0:T(8,128)(2,1)S(1)}, bf16[256,2048]{1,0:T(8,128)(2,1)}, u32[]{:S(2)}) copy-start(bf16[256,2048]{1,0:T(8,128)(2,1)} %param.27) | copy-start | bytes 3145732
  545.6 43.8 %copy-start.30 = (f32[2048]{0:T(1024)S(1)}, f32[2048]{0:T(1024)}, u32[]{:S(2)}) copy-start(f32[2048]{0:T(1024)} %param.23) | copy-start | bytes 24580
  545.6 43.8 %copy-start.34 = (f32[256]{0:T(256)S(1)}, f32[256]{0:T(256)}, u32[]{:S(2)}) copy-start(f32[256]{0:T(256)} %copy-done.33) | copy-start | bytes 3076
  545.6 43.8 %copy-start.38 = (f32[256]{0:T(256)S(1)}, f32[256]{0:T(256)}, u32[]{:S(2)}) copy-start(f32[256]{0:T(256)} %copy-done.37) | copy-start | bytes 3076
  (39 other events, 167.2 us)
Sparse Core Ops, SparseCore 0:
  11.6 37.1 all-gather.4
  100.4 44.4 reduce-scatter.6
  149.3 34.4 all-gather.6
  185.3 34.4 all-gather.8
  257.9 44.5 reduce-scatter.10
  307.9 34.4 all-gather.10
  491.7 44.4 reduce-scatter.12
  538.9 44.7 reduce-scatter.8
  587.4 95.6 reduce-scatter.14
  686.8 293.1 reduce-scatter.16
where the time goes:
time: 1000 us; the launch traced here: 995 us
  waiting for transfers between devices  586 us (59%)
  matrix products  201 us (20%)
  local copies, waits for them, and re-layouts  70.4 us (7%)
  other arithmetic  69.9 us (7%)
  blocking collectives  39.7 us (4%)
  between operations  15.7 us (2%)
  loops' own time  11.4 us (1%)
    reduce_scatter x1, waiting for transfers between devices, local(): lax.psum_scatter(ffn_terms.astype(jnp.bfloat16), 'dp', scatter_dimension=...  292 us
    reduce_scatter x1, waiting for transfers between devices, local(): lax.psum_scatter(attn_terms.astype(jnp.bfloat16), 'dp', scatter_dimension...  88.4 us
    dot_general x5, matrix products, dot_last(): lax.dot_general(left, right, (((1,), (1,)), ((), ())), preferred_element_...  48 us
    reduce_scatter x1, waiting for transfers between devices, local(): lax.psum_scatter((dot_last(grad_gate, w_gate) + dot_last(grad_up, w_up))....  44.6 us
    reduce_scatter x1, waiting for transfers between devices, local(): lax.psum_scatter(jnp.dot(attn_mixed, w_out, preferred_element_type=jnp.fl...  44.6 us
    dynamic_update_slice x4, local copies, waits for them, and re-layouts, local(): lax.map(attend_back, jnp.arange(block_total))  41.4 us
    psum x1, blocking collectives, local(): lax.psum((gain_one_grad, gain_two_grad), ('dp', 'row', 'col'))  39.7 us
    all_gather x1, waiting for transfers between devices, local(): lax.all_gather(grad_middle.astype(jnp.bfloat16), ('row', 'col'), axis=0,...  34.6 us
  transfers between devices with their start and end apart: 10, of which 8 were waited for; matrix products, arithmetic and copies ran while one was open for 9% of the time, Pallas kernels for 0%

commit v1 on v0

v1 whole, which is shorter than its diff:
```python
import jax
import jax.numpy as jnp
from jax import lax
from jax.experimental import pallas as pl
from jax.experimental.pallas import tpu as pltpu
from jax.sharding import PartitionSpec as P

HD = 64
EPSILON = 1e-05
MASKED_SCORE = -1e30
BLOCK = 256
TILE = 128
SWAP = ((0, 1), (1, 0))


def positions(segment_ids):
    indices = jnp.arange(segment_ids.shape[-1], dtype=jnp.int32)
    previous = jnp.concatenate([segment_ids[..., :1] - 1, segment_ids[..., :-1]], axis=-1)
    starts = jnp.where(segment_ids != previous, indices, 0)
    return indices - lax.cummax(starts, axis=segment_ids.ndim - 1)


def rope_tables(position):
    exponent = jnp.arange(HD // 2, dtype=jnp.float32) * (-2.0 / HD)
    angles = position.astype(jnp.float32)[:, None] * (10000.0**exponent)[None, :]
    cosine, sine = jnp.cos(angles), jnp.sin(angles)
    return (
        jnp.concatenate([cosine] * 4, axis=1),
        jnp.concatenate([-sine, sine, -sine, sine], axis=1),
    )


def nt(left, right):
    return lax.dot_general(
        left, right, (((1,), (1,)), ((), ())), preferred_element_type=jnp.float32
    )


def nn(left, right):
    return lax.dot_general(
        left, right, (((1,), (0,)), ((), ())), preferred_element_type=jnp.float32
    )


def tn(left, right):
    return lax.dot_general(
        left, right, (((0,), (0,)), ((), ())), preferred_element_type=jnp.float32
    )


def lane_marks():
    lane = lax.broadcasted_iota(jnp.int32, (BLOCK, TILE), 1)
    return lane, lane < HD, lane % HD < HD // 2


def turn_by(values, cosine, sine, first):
    turned = jnp.where(
        first, pltpu.roll(values, TILE - HD // 2, 1), pltpu.roll(values, HD // 2, 1)
    )
    return values * cosine + turned * sine


def rows_of(places, block):
    return pl.ds(pl.multiple_of(places[block], BLOCK), BLOCK)


def attend_kernel(
    places, proj, cosine, sine, seg_col, seg_row, mixed, rotated, log_sums, keys, values
):
    length = proj.shape[0]
    width = mixed.shape[1]
    blocks = length // BLOCK
    lane, low, first = lane_marks()
    for block in range(blocks):
        rows = rows_of(places, block)
        at = slice(block * BLOCK, (block + 1) * BLOCK)
        pair = proj[rows, width:]
        turned = jnp.where(low, turn_by(pair, cosine[at], sine[at], first), pair)
        swapped = pltpu.roll(turned, HD, 1)
        rotated[rows, width:] = turned.astype(jnp.bfloat16)
        keys[at] = jnp.where(low, turned, swapped).astype(jnp.bfloat16)
        values[at] = jnp.where(low, swapped, turned).astype(jnp.bfloat16)
    for block in range(blocks):
        rows = rows_of(places, block)
        at = slice(block * BLOCK, (block + 1) * BLOCK)
        begin = max(0, block - 2) * BLOCK
        span = slice(begin, (block + 1) * BLOCK)
        count = (block + 1) * BLOCK - begin
        key_at = begin + lax.broadcasted_iota(jnp.int32, (BLOCK, count), 1)
        query_at = block * BLOCK + lax.broadcasted_iota(jnp.int32, (BLOCK, count), 0)
        allowed = (seg_col[at] == seg_row[:, span]) & (key_at <= query_at)
        bias = jnp.where(allowed, 0.0, MASKED_SCORE)
        key_span = keys[span]
        value_span = values[span]

        def one_pair(number, logs):
            columns = pl.ds(pl.multiple_of(number * TILE, TILE), TILE)
            query = turn_by(proj[rows, columns], cosine[at], sine[at], first) * HD ** (-0.5)
            query = query.astype(jnp.bfloat16)
            rotated[rows, columns] = query
            results = []
            for half in range(2):
                chosen = jnp.where(low if half == 0 else ~low, query, jnp.zeros_like(query))
                scores = nt(chosen, key_span) + bias
                largest = jnp.max(scores, axis=1, keepdims=True)
                shifted = jnp.exp(scores - largest)
                total = jnp.sum(shifted, axis=1, keepdims=True)
                results.append(nn(shifted.astype(jnp.bfloat16), value_span) * (1.0 / total))
                logs = jnp.where(lane == 2 * number + half, largest + jnp.log(total), logs)
            mixed[rows, columns] = jnp.where(low, results[0], results[1]).astype(jnp.bfloat16)
            return logs

        logs = lax.fori_loop(0, width // TILE, one_pair, jnp.zeros((BLOCK, TILE), jnp.float32))
        log_sums[:, at] = logs.T[: log_sums.shape[0]]


def attend_back_kernel(
    places,
    rotated,
    grad_mixed,
    log_sums,
    cosine,
    sine,
    seg_col,
    seg_row,
    grads,
    keys,
    values,
    key_sum,
    value_sum,
):
    length = rotated.shape[0]
    width = grad_mixed.shape[1]
    blocks = length // BLOCK
    _, low, first = lane_marks()
    key_sum[...] = jnp.zeros_like(key_sum)
    value_sum[...] = jnp.zeros_like(value_sum)
    for block in range(blocks):
        rows = rows_of(places, block)
        at = slice(block * BLOCK, (block + 1) * BLOCK)
        pair = rotated[rows, width:].astype(jnp.float32)
        swapped = pltpu.roll(pair, HD, 1)
        keys[at] = jnp.where(low, pair, swapped).astype(jnp.bfloat16)
        values[at] = jnp.where(low, swapped, pair).astype(jnp.bfloat16)
    for block in range(blocks):
        rows = rows_of(places, block)
        at = slice(block * BLOCK, (block + 1) * BLOCK)
        begin = max(0, block - 2) * BLOCK
        span = slice(begin, (block + 1) * BLOCK)
        count = (block + 1) * BLOCK - begin
        key_at = begin + lax.broadcasted_iota(jnp.int32, (count, BLOCK), 0)
        query_at = block * BLOCK + lax.broadcasted_iota(jnp.int32, (count, BLOCK), 1)
        allowed = (seg_col[span] == seg_row[:, at]) & (key_at <= query_at)
        bias = jnp.where(allowed, 0.0, MASKED_SCORE)
        key_span = keys[span]
        value_span = values[span]

        def one_pair(number, carry):
            columns = pl.ds(pl.multiple_of(number * TILE, TILE), TILE)
            query = rotated[rows, columns]
            grad = grad_mixed[rows, columns]
            results = []
            for half in range(2):
                side = low if half == 0 else ~low
                chosen = jnp.where(side, query, jnp.zeros_like(query))
                chosen_grad = jnp.where(side, grad, jnp.zeros_like(grad))
                logs = log_sums[pl.ds(2 * number + half, 1), at]
                probs = jnp.exp(nt(key_span, chosen) + bias - logs)
                grad_probs = nt(value_span, chosen_grad)
                inner = jnp.sum(probs * grad_probs, axis=0, keepdims=True)
                grad_scores = (probs * (grad_probs - inner)).astype(jnp.bfloat16)
                value_sum[span] += nn(probs.astype(jnp.bfloat16), chosen_grad)
                key_sum[span] += nn(grad_scores, chosen)
                results.append(tn(grad_scores, key_span))
            grad_query = jnp.where(low, results[0], results[1]) * HD ** (-0.5)
            grads[rows, columns] = turn_by(grad_query, cosine[at], -sine[at], first).astype(
                jnp.bfloat16
            )
            return carry

        lax.fori_loop(0, width // TILE, one_pair, 0)
    for block in range(blocks):
        rows = rows_of(places, block)
        at = slice(block * BLOCK, (block + 1) * BLOCK)
        grad_key = key_sum[at]
        grad_key = turn_by(grad_key + pltpu.roll(grad_key, HD, 1), cosine[at], -sine[at], first)
        grad_value = value_sum[at]
        grad_value = grad_value + pltpu.roll(grad_value, HD, 1)
        grads[rows, width:] = jnp.where(low, grad_key, grad_value).astype(jnp.bfloat16)


SMEM = pl.BlockSpec(memory_space=pltpu.SMEM)
VMEM = pl.BlockSpec(memory_space=pltpu.VMEM)


def attend(places, proj, cosine, sine, seg_col, seg_row):
    length, total = proj.shape
    width = total - TILE
    return pl.pallas_call(
        attend_kernel,
        out_shape=(
            jax.ShapeDtypeStruct((length, width), jnp.bfloat16),
            jax.ShapeDtypeStruct((length, total), jnp.bfloat16),
            jax.ShapeDtypeStruct((width // HD, length), jnp.float32),
        ),
        in_specs=[SMEM] + [VMEM] * 5,
        out_specs=(VMEM,) * 3,
        scratch_shapes=[pltpu.VMEM((length, TILE), jnp.bfloat16)] * 2,
        compiler_params=pltpu.CompilerParams(vmem_limit_bytes=48 << 20),
        cost_estimate=pl.CostEstimate(
            flops=17 << 30, bytes_accessed=8 << 20, transcendentals=0
        ),
    )(places, proj, cosine, sine, seg_col, seg_row)


def attend_back(places, rotated, grad_mixed, log_sums, cosine, sine, seg_col, seg_row):
    length, total = rotated.shape
    return pl.pallas_call(
        attend_back_kernel,
        out_shape=jax.ShapeDtypeStruct((length, total), jnp.bfloat16),
        in_specs=[SMEM] + [VMEM] * 7,
        out_specs=VMEM,
        scratch_shapes=[pltpu.VMEM((length, TILE), jnp.bfloat16)] * 2
        + [pltpu.VMEM((length, TILE), jnp.float32)] * 2,
        compiler_params=pltpu.CompilerParams(vmem_limit_bytes=48 << 20),
        cost_estimate=pl.CostEstimate(
            flops=26 << 30, bytes_accessed=8 << 20, transcendentals=0
        ),
    )(places, rotated, grad_mixed, log_sums, cosine, sine, seg_col, seg_row)


def to_core(values):
    return lax.ppermute(values, "row", SWAP)


def to_chip(values):
    return lax.ppermute(values, "col", SWAP)


def gather_blocks(own):
    across = to_chip(own)
    return own, to_core(own), across, to_core(across)


def scatter_blocks(products):
    own, beside, across, diagonal = products
    across_sum = (across + to_core(diagonal.astype(jnp.bfloat16))).astype(jnp.bfloat16)
    return own + to_core(beside.astype(jnp.bfloat16)) + to_chip(across_sum)


def pick(values, index, axis):
    return lax.dynamic_index_in_dim(values, index, axis, keepdims=False)


def halve_inner(values, line, inner, index, dp):
    while inner > 1:
        half = inner // 2
        bit = (index // half) % 2
        values = values.reshape((line, 2, half) + values.shape[2:])
        swaps = [(device, device ^ half) for device in range(dp)]
        arrived = lax.ppermute(pick(values, 1 - bit, 1), "dp", swaps)
        values = (pick(values, bit, 1) + arrived).astype(jnp.bfloat16)
        inner = half
    return values.reshape((line,) + values.shape[2:])


def along_line(values, line, inner, index):
    place = index // inner
    up = down = None
    for step in range(1, line):
        upward = pick(values, jnp.clip(line - step + place, 0, line - 1), 0)
        downward = pick(values, jnp.clip(place + step - line, 0, line - 1), 0)
        if step > 1:
            upward = upward + up
            downward = downward + down
        up_pairs, down_pairs = [], []
        for at in range(line - 1):
            if at < step:
                for low in range(inner):
                    up_pairs.append((at * inner + low, (at + 1) * inner + low))
                    mirror = line - 1 - at
                    down_pairs.append((mirror * inner + low, (mirror - 1) * inner + low))
        up = lax.ppermute(upward, "dp", up_pairs)
        down = lax.ppermute(downward, "dp", down_pairs)
    mine = pick(values, place, 0).astype(jnp.float32)
    return mine + up.astype(jnp.float32) + down.astype(jnp.float32)


def sum_over_dp(values, sizes, line_first):
    dp, line, inner = sizes
    index = lax.axis_index("dp")
    rows, columns = values.shape
    blocks = values.reshape(line, inner, rows // dp, columns)
    if not line_first:
        return along_line(halve_inner(blocks, line, inner, index, dp), line, inner, index)
    part = along_line(blocks, line, inner, index).astype(jnp.bfloat16)
    return halve_inner(part[None], 1, inner, index, dp)[0].astype(jnp.float32)


def sum_everywhere(values, dp):
    values = values + to_core(values)
    values = values + to_chip(values)
    step = 1
    while step < dp:
        values = values + lax.ppermute(values, "dp", [(i, i ^ step) for i in range(dp)])
        step *= 2
    return values


def norm_back(grad_normed, unit_rows, inverse, gain):
    scaled = grad_normed * gain
    inner = jnp.mean(scaled * unit_rows, axis=-1, keepdims=True)
    return inverse * (scaled - unit_rows * inner), jnp.sum(grad_normed * unit_rows, axis=0)


def local_for(dp):
    line = 4 if dp % 4 == 0 else 1
    sizes = (dp, line, dp // line)

    def local(
        tokens,
        segments,
        attn_gain,
        w_query,
        w_key,
        w_value,
        w_out,
        ffn_gain,
        w_gate,
        w_up,
        w_down,
        out_cotangent,
    ):
        query_width = w_query.shape[1]
        kv_width = w_key.shape[1]
        length = segments.shape[1]
        row, col = lax.axis_index("row"), lax.axis_index("col")
        places = jnp.stack(
            [((block // 2) ^ row) + 2 * ((block % 2) ^ col) for block in range(4)]
        ) * (length // 4)
        places = places.astype(jnp.int32)
        cosine, sine = rope_tables(positions(segments).reshape(length))
        seg_col = segments.reshape(length, 1)
        seg_row = segments.reshape(1, length)
        qkv_weight = jnp.concatenate([w_query, w_key, w_value], axis=1)

        inputs = tokens.astype(jnp.float32)
        inverse_one = lax.rsqrt(jnp.mean(inputs * inputs, axis=-1, keepdims=True) + EPSILON)
        unit_one = inputs * inverse_one
        normed_one = (unit_one * attn_gain).astype(jnp.bfloat16)
        blocks_one = gather_blocks(normed_one)
        proj = jnp.concatenate([nn(block, qkv_weight) for block in blocks_one], axis=0)
        attn_mixed, rotated, log_sums = attend(places, proj, cosine, sine, seg_col, seg_row)
        rows = length // 4
        mixed_blocks = [attn_mixed[i * rows : (i + 1) * rows] for i in range(4)]
        middle = inputs + scatter_blocks([nn(block, w_out) for block in mixed_blocks])

        cot_blocks = gather_blocks(out_cotangent)
        grad_rows = jnp.concatenate(cot_blocks, axis=0)
        inverse_two = lax.rsqrt(jnp.mean(middle * middle, axis=-1, keepdims=True) + EPSILON)
        unit_two = middle * inverse_two
        normed_two = (unit_two * ffn_gain).astype(jnp.bfloat16)
        gathered_two = jnp.concatenate(gather_blocks(normed_two), axis=0)
        gate_pre = nn(gathered_two, w_gate)
        up_pre = nn(gathered_two, w_up)
        sigmoid_gate = jax.nn.sigmoid(gate_pre)
        hidden = (gate_pre * sigmoid_gate * up_pre).astype(jnp.bfloat16)
        down_grad = sum_over_dp(tn(grad_rows, hidden).astype(jnp.bfloat16), sizes, False)
        grad_hidden = nt(grad_rows, w_down)
        slope = sigmoid_gate + gate_pre * sigmoid_gate * (1.0 - sigmoid_gate)
        grad_gate = (grad_hidden * up_pre * slope).astype(jnp.bfloat16)
        grad_up = (grad_hidden * gate_pre * sigmoid_gate).astype(jnp.bfloat16)
        gate_grad = sum_over_dp(tn(gathered_two, grad_gate).astype(jnp.bfloat16), sizes, True)
        up_grad = sum_over_dp(tn(gathered_two, grad_up).astype(jnp.bfloat16), sizes, False)

        back_two = nt(grad_gate, w_gate) + nt(grad_up, w_up)
        grad_normed_two = scatter_blocks([back_two[i * rows : (i + 1) * rows] for i in range(4)])
        grad_middle_norm, gain_two_grad = norm_back(
            grad_normed_two, unit_two, inverse_two, ffn_gain
        )
        grad_middle = out_cotangent.astype(jnp.float32) + grad_middle_norm
        grad_attn_blocks = gather_blocks(grad_middle.astype(jnp.bfloat16))
        grad_mixed = jnp.concatenate(
            [nt(block, w_out).astype(jnp.bfloat16) for block in grad_attn_blocks], axis=0
        )
        out_terms = jnp.concatenate(grad_attn_blocks, axis=0)
        out_grad = sum_over_dp(tn(out_terms, attn_mixed).astype(jnp.bfloat16), sizes, False)
        down = nn(hidden, w_down)
        output = middle + scatter_blocks([down[i * rows : (i + 1) * rows] for i in range(4)])

        grad_qkv = attend_back(
            places, rotated, grad_mixed, log_sums, cosine, sine, seg_col, seg_row
        )
        qkv_terms = tn(jnp.concatenate(blocks_one, axis=0), grad_qkv)
        gain_one_grad = jnp.sum(qkv_terms * qkv_weight.astype(jnp.float32), axis=1) / attn_gain
        qkv_grad = sum_over_dp(qkv_terms.astype(jnp.bfloat16), sizes, False)
        back_one = nt(grad_qkv, qkv_weight)
        grad_normed_one = scatter_blocks([back_one[i * rows : (i + 1) * rows] for i in range(4)])
        scaled = grad_normed_one * attn_gain
        inner = jnp.mean(scaled * unit_one, axis=-1, keepdims=True)
        input_grad = grad_middle + inverse_one * (scaled - unit_one * inner)
        gains = sum_everywhere(jnp.stack([gain_one_grad, gain_two_grad]), dp)
        key_end = query_width + kv_width
        return (
            output.astype(jnp.bfloat16),
            input_grad,
            gains[0],
            qkv_grad[:, :query_width],
            qkv_grad[:, query_width:key_end],
            qkv_grad[:, key_end:],
            out_grad.T,
            gains[1],
            gate_grad,
            up_grad,
            down_grad.T,
        )

    return local


def solution(mesh):
    rows = P(("dp", "row", "col"), None)
    columns = P(None, ("row", "col"))
    placed = (
        rows,
        P("dp", None),
        P(),
        columns,
        columns,
        columns,
        P(("row", "col"), None),
        P(),
        columns,
        columns,
        P(("row", "col"), None),
        rows,
    )
    summed = P("dp", ("row", "col"))
    turned = P(("row", "col"), "dp")
    return jax.shard_map(
        local_for(mesh.shape["dp"]),
        mesh=mesh,
        in_specs=placed,
        out_specs=(rows, rows, P(), summed, summed, summed, turned, P(), summed, summed, turned),
        check_vma=False,
    )
```

time: 1000 us -> 619 us (0.62)
  waiting for transfers between devices: 586 us -> 199 us
  starting transfers between devices: 0.41 us -> 132 us
  matrix products: 201 us -> 134 us
  Pallas kernels: 0 us -> 42.2 us
  blocking collectives: 39.7 us -> 0 us
  local copies, waits for them, and re-layouts: 70.4 us -> 49.7 us
  other arithmetic: 69.9 us -> 51.7 us
  between operations: 15.7 us -> 2.98 us
  loops' own time: 11.4 us -> 0 us
    reduce_scatter x6 -> x0, waiting for transfers between devices: 469 us -> none  [the longest x1 292 us: local(): lax.psum_scatter(ffn_terms.astype(jnp.bfloat16), 'dp', scatter_dimension=...]
    ppermute x0 -> x64, waiting for transfers between devices: none -> 199 us  [the longest x9 122 us: to_chip(): return lax.ppermute(values, 'col', SWAP)]
    ppermute x0 -> x64, starting transfers between devices: none -> 132 us  [the longest x15 92.4 us: along_line(): up = lax.ppermute(upward, 'dp', up_pairs)]
    all_gather x4 -> x0, waiting for transfers between devices: 116 us -> none  [the longest x1 34.6 us: local(): lax.all_gather(grad_middle.astype(jnp.bfloat16), ('row', 'col'), axis=0,...]
    dot_general x29 -> x24, matrix products: 201 us -> 134 us  [the longest x11 49.7 us: nn(): lax.dot_general(left, right, (((1,), (0,)), ((), ())), preferred_element_...]
    dynamic_update_slice x8 -> x0, local copies, waits for them, and re-layouts: 43.4 us -> none  [the longest x4 41.4 us: local(): lax.map(attend_back, jnp.arange(block_total))]
    pallas_call x0 -> x2, Pallas kernels: none -> 42.2 us  [the longest x1 24.3 us: attend_back(): pl.pallas_call(attend_back_kernel, out_shape=jax.ShapeDtypeStruct((length...]
    psum x1 -> x0, blocking collectives: 39.7 us -> none  [local(): lax.psum((gain_one_grad, gain_two_grad), ('dp', 'row', 'col'))]
  transfers between devices with their start and end apart: 10 -> 64, of which waited for: 8 -> 21; matrix products, arithmetic and copies ran while one was open for 9% -> 25% of each run, Pallas kernels for 0% -> 4%
where the time goes in v1:
time: 619 us; the launch traced here: 611 us
  waiting for transfers between devices  199 us (32%)
  matrix products  134 us (22%)
  starting transfers between devices  132 us (21%)
  other arithmetic  51.7 us (8%)
  local copies, waits for them, and re-layouts  49.7 us (8%)
  Pallas kernels  42.2 us (7%)
    ppermute x9, waiting for transfers between devices, to_chip(): return lax.ppermute(values, 'col', SWAP)  122 us
    ppermute x15, starting transfers between devices, along_line(): up = lax.ppermute(upward, 'dp', up_pairs)  92.4 us
    dot_general x11, matrix products, nn(): lax.dot_general(left, right, (((1,), (0,)), ((), ())), preferred_element_...  49.7 us
    dot_general x8, matrix products, nt(): lax.dot_general(left, right, (((1,), (1,)), ((), ())), preferred_element_...  47.8 us
    dot_general x5, matrix products, tn(): lax.dot_general(left, right, (((0,), (0,)), ((), ())), preferred_element_...  36.3 us
    ppermute x15, waiting for transfers between devices, along_line(): down = lax.ppermute(downward, 'dp', down_pairs)  32.1 us
    ppermute x15, waiting for transfers between devices, along_line(): up = lax.ppermute(upward, 'dp', up_pairs)  30.3 us
    pallas_call x1, Pallas kernels, attend_back(): pl.pallas_call(attend_back_kernel, out_shape=jax.ShapeDtypeStruct((length...  24.3 us
  transfers between devices with their start and end apart: 64, of which 21 were waited for; matrix products, arithmetic and copies ran while one was open for 25% of the time, Pallas kernels for 4%

profile of v1, /device:TPU:0, one launch (start us, length us, event | category | flops | bytes accessed | tf_op | source)
XLA Modules:
  0.0 610.8 jit_solution(18200364133279015310)
XLA Ops:
  16.6 14.7 %collective-permute-done.1 = bf16[256,2048]{1,0:T(8,128)(2,1)} collective-permute-done((bf16[256,2048]{1,0:T(8,128)(2,1)}, bf16[256,2048]{1,0:T(8,128)(2,1)}, u32[]{:S(2)}, u32[]{:S(2)}) %collective-permute-start.1) | collective-permute-done | bytes 1048608 | tf_op jit(solution)/shard_map/ppermute | solution.py:237
  44.0 18.0 %shard_map.203 = (bf16[1024,512]{1,0:T(8,128)(2,1)S(1)}, bf16[1024,640]{1,0:T(8,128)(2,1)S(1)}, f32[8,1024]{1,0:T(8,128)S(1)}) custom-call(s32[4]{0:T(128)S(1)} %add_multiply_fusion.places, f32[1024,640]{1,0:T(8,128)} %pad_maximum_fusion.2.proj, f32[1024,128]{1,0:T(8,128)S(1)} %get-tuple-element.107.cosine, f32[1024,128]{1,0:T(8,128)S(1)} %get-tuple-element.108.sine, ...), custom_call_target="tpu_custom_call" | custom-call | flops 18253611008 | bytes 8388608 | tf_op jit(solution)/shard_map/pallas_call | solution.py:199
  69.3 23.2 %collective-permute-done.5 = bf16[256,2048]{1,0:T(8,128)(2,1)S(1)} collective-permute-done((bf16[256,2048]{1,0:T(8,128)(2,1)S(1)}, bf16[256,2048]{1,0:T(8,128)(2,1)S(1)}, u32[]{:S(2)}, u32[]{:S(2)}) %collective-permute-start.5) | collective-permute-done | bytes 1048608 | tf_op jit(solution)/shard_map/ppermute | solution.py:237
  97.5 17.6 %collective-permute-done.13 = bf16[256,2048]{1,0:T(8,128)(2,1)} collective-permute-done((bf16[256,2048]{1,0:T(8,128)(2,1)}, bf16[256,2048]{1,0:T(8,128)(2,1)}, u32[]{:S(2)}, u32[]{:S(2)}) %collective-permute-start.13) | collective-permute-done | bytes 1048608 | tf_op jit(solution)/shard_map/ppermute | solution.py:237
  115.5 21.4 %collective-permute-done.7 = bf16[256,2048]{1,0:T(8,128)(2,1)} collective-permute-done((bf16[256,2048]{1,0:T(8,128)(2,1)}, bf16[256,2048]{1,0:T(8,128)(2,1)}, u32[]{:S(2)}, u32[]{:S(2)}) %collective-permute-start.7) | collective-permute-done | bytes 1048608 | tf_op jit(solution)/shard_map/ppermute | solution.py:237
  142.4 13.0 %fusion.60 = f32[1024,1408]{1,0:T(8,128)} fusion(bf16[2048,1408]{1,0:T(8,128)(2,1)} %param.21, bf16[256,2048]{1,0:T(8,128)(2,1)} %collective-permute-done.8, bf16[256,2048]{1,0:T(8,128)(2,1)} %collective-permute-done.7, bf16[256,2048]{1,0:T(8,128)(2,1)} %collective-permute-done.6, bf16[256,2048]{1,0:T(8,128)(2,1)} %multiply_convert_fusion.3), kind=kOutput, calls=%fused_computation.158 | convolution fusion | flops 5922357248 | bytes 15728640 | tf_op jit(solution)/shard_map/dot_general | solution.py:40
  155.3 11.5 %fusion.61 = f32[1024,1408]{1,0:T(8,128)} fusion(bf16[2048,1408]{1,0:T(8,128)(2,1)S(1)} %bitcast.198, bf16[256,2048]{1,0:T(8,128)(2,1)} %collective-permute-done.8, bf16[256,2048]{1,0:T(8,128)(2,1)} %collective-permute-done.7, bf16[256,2048]{1,0:T(8,128)(2,1)} %collective-permute-done.6, bf16[256,2048]{1,0:T(8,128)(2,1)} %multiply_convert_fusion.3), kind=kOutput, calls=%fused_computation.159 | convolution fusion | flops 5922357248 | bytes 15728640 | tf_op jit(solution)/shard_map/dot_general | solution.py:40
  166.9 14.5 %multiply_convert_fusion = (bf16[1024,1408]{1,0:T(8,128)(2,1)}, bf16[1024,1408]{1,0:T(8,128)(2,1)}, bf16[1024,1408]{1,0:T(8,128)(2,1)S(1)}) fusion(f32[1024,1408]{1,0:T(8,128)} %fusion.61, f32[1024,1408]{1,0:T(8,128)} %fusion.60, bf16[1024,2048]{1,0:T(8,128)(2,1)S(1)} %constant_dynamic-update-slice_fusion, bf16[1408,2048]{1,0:T(8,128)(2,1)} %param.22), kind=kOutput, calls=%fused_computation.3 | convolution fusion | flops 5927206912 | bytes 30146560 | tf_op jit(solution)/shard_map/dot_general | solution.py:34
  188.4 12.4 %fusion.70 = (bf16[1024,2048]{1,0:T(8,128)(2,1)}, f32[1024,2048]{1,0:T(8,128)}) fusion(bf16[1024,1408]{1,0:T(8,128)(2,1)S(1)} %get-tuple-element.58, bf16[1408,2048]{1,0:T(8,128)(2,1)} %param.22), kind=kOutput, calls=%fused_computation.168 | convolution fusion | flops 5907677184 | bytes 21233664 | tf_op jit(solution)/shard_map/dot_general | solution.py:40
  210.1 12.1 %fusion.76 = f32[1024,2048]{1,0:T(8,128)} fusion(bf16[1024,1408]{1,0:T(8,128)(2,1)} %get-tuple-element.57, bf16[2048,1408]{1,0:T(8,128)(2,1)} %param.20), kind=kOutput, calls=%fused_computation.174 | convolution fusion | flops 5905580032 | bytes 17039360 | tf_op jit(solution)/shard_map/dot_general | solution.py:34
  222.2 8.7 %convolution_convert_fusion.2 = bf16[2048,1408]{1,0:T(8,128)(2,1)S(1)} fusion(bf16[1024,1408]{1,0:T(8,128)(2,1)S(1)} %copy-done.40, bf16[256,2048]{1,0:T(8,128)(2,1)} %collective-permute-done.8, bf16[256,2048]{1,0:T(8,128)(2,1)} %collective-permute-done.7, bf16[256,2048]{1,0:T(8,128)(2,1)} %collective-permute-done.6, ...), kind=kOutput, calls=%fused_computation.2 | convolution fusion | flops 5925240832 | bytes 12845056 | tf_op jit(solution)/shard_map/dot_general | solution.py:46
  241.7 11.1 %fusion.69 = (bf16[1024,2048]{1,0:T(8,128)(2,1)S(1)}, f32[1024,2048]{1,0:T(8,128)}) fusion(f32[1024,2048]{1,0:T(8,128)} %fusion.76, bf16[1024,1408]{1,0:T(8,128)(2,1)S(1)} %copy-done.39, bf16[2048,1408]{1,0:T(8,128)(2,1)S(1)} %bitcast.200), kind=kOutput, calls=%fused_computation.167 | convolution fusion | flops 5909774336 | bytes 29622272 | tf_op jit(solution)/shard_map/dot_general | solution.py:34
  254.8 10.9 %convolution_convert_fusion.1 = bf16[2048,1408]{1,0:T(8,128)(2,1)} fusion(bf16[1024,1408]{1,0:T(8,128)(2,1)S(1)} %copy-done.39, bf16[256,2048]{1,0:T(8,128)(2,1)} %collective-permute-done.8, bf16[256,2048]{1,0:T(8,128)(2,1)} %collective-permute-done.7, bf16[256,2048]{1,0:T(8,128)(2,1)} %collective-permute-done.6, bf16[256,2048]{1,0:T(8,128)(2,1)} %multiply_convert_fusion.3), kind=kOutput, calls=%fused_computation.1 | convolution fusion | flops 5925240832 | bytes 12845056 | tf_op jit(solution)/shard_map/dot_general | solution.py:46
  282.5 18.8 %collective-permute-done.17 = bf16[256,2048]{1,0:T(8,128)(2,1)S(1)} collective-permute-done((bf16[256,2048]{1,0:T(8,128)(2,1)S(1)}, bf16[256,2048]{1,0:T(8,128)(2,1)S(1)}, u32[]{:S(2)}, u32[]{:S(2)}) %collective-permute-start.17) | collective-permute-done | bytes 1048608 | tf_op jit(solution)/shard_map/ppermute | solution.py:237
  306.0 17.6 %collective-permute-done.11 = bf16[256,2048]{1,0:T(8,128)(2,1)} collective-permute-done((bf16[256,2048]{1,0:T(8,128)(2,1)S(1)}, bf16[256,2048]{1,0:T(8,128)(2,1)}, u32[]{:S(2)}, u32[]{:S(2)}) %collective-permute-start.11) | collective-permute-done | bytes 1048608 | tf_op jit(solution)/shard_map/ppermute | solution.py:237
  345.7 9.0 %collective-permute-done.19 = bf16[256,2048]{1,0:T(8,128)(2,1)S(1)} collective-permute-done((bf16[256,2048]{1,0:T(8,128)(2,1)}, bf16[256,2048]{1,0:T(8,128)(2,1)S(1)}, u32[]{:S(2)}, u32[]{:S(2)}) %collective-permute-start.19) | collective-permute-done | bytes 1048608 | tf_op jit(solution)/shard_map/ppermute | solution.py:237
  360.6 9.1 %collective-permute-done.51 = bf16[256,1408]{1,0:T(8,128)(2,1)S(1)} collective-permute-done((bf16[256,1408]{1,0:T(8,128)(2,1)S(1)}, bf16[256,1408]{1,0:T(8,128)(2,1)S(1)}, u32[]{:S(2)}, u32[]{:S(2)}) %collective-permute-start.51) | collective-permute-done | bytes 720928 | tf_op jit(solution)/shard_map/ppermute | solution.py:283
  377.4 24.3 %shard_map.204 = bf16[1024,640]{1,0:T(8,128)(2,1)S(1)} custom-call(s32[4]{0:T(128)S(1)} %add_multiply_fusion.places, bf16[1024,640]{1,0:T(8,128)(2,1)S(1)} %copy-done.7, bf16[1024,512]{1,0:T(8,128)(2,1)S(1)} %pad_maximum_fusion.3.grad_mixed, f32[8,1024]{1,0:T(8,128)S(1)} %get-tuple-element.16.log_sums, f32[1024,128]{1,0:T(8,128)S(1)} %get-tuple-element.107.cosine, ...), custom_call_target="tpu_custom_call" | custom-call | flops 27917287424 | bytes 8388608 | tf_op jit(solution)/shard_map/pallas_call | solution.py:218
  461.0 9.5 %collective-permute-done.36 = bf16[4,1,256,512]{2,3,1,0:T(8,128)(2,1)S(1)} collective-permute-done((bf16[4,1,256,512]{2,3,1,0:T(8,128)(2,1)}, bf16[4,1,256,512]{2,3,1,0:T(8,128)(2,1)S(1)}, u32[]{:S(2)}, u32[]{:S(2)}) %collective-permute-start.36) | collective-permute-done | bytes 1048608 | tf_op jit(solution)/shard_map/ppermute | solution.py:261
  471.9 20.5 %collective-permute-start.37 = (bf16[256,512]{0,1:T(8,128)(2,1)S(1)}, bf16[256,512]{0,1:T(8,128)(2,1)S(1)}, u32[]{:S(2)}, u32[]{:S(2)}) collective-permute-start(bf16[256,512]{0,1:T(8,128)(2,1)S(1)} %get-tuple-element.92), channel_id=1, source_target_pairs={{0,8},{4,12},{1,9},{5,13},{2,10},{6,14},{3,11},{7,15}} | collective-permute-start | bytes 786440 | tf_op jit(solution)/shard_map/ppermute | solution.py:283
  510.3 25.0 %collective-permute-start.53 = (bf16[256,1408]{1,0:T(8,128)(2,1)S(1)}, bf16[256,1408]{1,0:T(8,128)(2,1)S(1)}, u32[]{:S(2)}, u32[]{:S(2)}) collective-permute-start(bf16[256,1408]{1,0:T(8,128)(2,1)S(1)} %get-tuple-element.77), channel_id=1, source_target_pairs={{0,8},{4,12},{8,16},{12,20},{16,24},{20,28},{1,9},{5,13},{9,17},{1... | collective-permute-start | bytes 2162696 | tf_op jit(solution)/shard_map/ppermute | solution.py:283
  540.6 15.8 %collective-permute-done.63 = bf16[256,1408]{0,1:T(8,128)(2,1)S(1)} collective-permute-done((bf16[256,1408]{0,1:T(8,128)(2,1)S(1)}, bf16[256,1408]{0,1:T(8,128)(2,1)S(1)}, u32[]{:S(2)}, u32[]{:S(2)}) %collective-permute-start.63) | collective-permute-done | bytes 720928 | tf_op jit(solution)/shard_map/ppermute | solution.py:284
  582.3 9.3 %collective-permute-start.32 = (bf16[256,640]{0,1:T(8,128)(2,1)S(1)}, bf16[256,640]{0,1:T(8,128)(2,1)S(1)}, u32[]{:S(2)}, u32[]{:S(2)}) collective-permute-start(bf16[256,640]{0,1:T(8,128)(2,1)S(1)} %get-tuple-element.86), channel_id=1, source_target_pairs={{0,8},{4,12},{8,16},{12,20},{16,24},{20,28},{1,9},{5,13},{9,17},{1... | collective-permute-start | bytes 983048 | tf_op jit(solution)/shard_map/ppermute | solution.py:283
  598.1 10.7 %collective-permute-done.35 = bf16[256,640]{0,1:T(8,128)(2,1)S(1)} collective-permute-done((bf16[256,640]{0,1:T(8,128)(2,1)S(1)}, bf16[256,640]{0,1:T(8,128)(2,1)S(1)}, u32[]{:S(2)}, u32[]{:S(2)}) %collective-permute-start.35) | collective-permute-done | bytes 327712 | tf_op jit(solution)/shard_map/ppermute | solution.py:284
  (329 shorter events, 249.3 us)
Async XLA Ops:
  7.9 30.0 %collective-permute-start = (bf16[256,2048]{1,0:T(8,128)(2,1)}, bf16[256,2048]{1,0:T(8,128)(2,1)}, u32[]{:S(2)}, u32[]{:S(2)}) collective-permute-start(bf16[256,2048]{1,0:T(8,128)(2,1)} %fusion.25), channel_id=1, source_target_pairs={{0,2},{2,0},{1,3},{3,1},{4,6},{6,4},{5,7},{7,5},{8,10},{10,8},{9,1... | collective-permute-start | bytes 3145736 | tf_op jit(solution)/shard_map/ppermute | solution.py:233
  68.2 46.8 %collective-permute-start.13 = (bf16[256,2048]{1,0:T(8,128)(2,1)}, bf16[256,2048]{1,0:T(8,128)(2,1)}, u32[]{:S(2)}, u32[]{:S(2)}) collective-permute-start(bf16[256,2048]{1,0:T(8,128)(2,1)} %param.23), channel_id=1, source_target_pairs={{0,1},{1,0},{2,3},{3,2},{4,5},{5,4},{6,7},{7,6},{8,9},{9,8},{10,11... | collective-permute-start | bytes 3145736 | tf_op jit(solution)/shard_map/ppermute | solution.py:237
  95.7 41.2 %collective-permute-start.7 = (bf16[256,2048]{1,0:T(8,128)(2,1)}, bf16[256,2048]{1,0:T(8,128)(2,1)}, u32[]{:S(2)}, u32[]{:S(2)}) collective-permute-start(bf16[256,2048]{1,0:T(8,128)(2,1)} %multiply_convert_fusion.3), channel_id=1, source_target_pairs={{0,1},{1,0},{2,3},{3,2},{4,5},{5,4},{6,7},{7,6},{8,9},{9,8},{10,11... | collective-permute-start | bytes 3145736 | tf_op jit(solution)/shard_map/ppermute | solution.py:237
  97.5 40.8 %collective-permute-start.12 = (bf16[256,2048]{1,0:T(8,128)(2,1)}, bf16[256,2048]{1,0:T(8,128)(2,1)}, u32[]{:S(2)}, u32[]{:S(2)}) collective-permute-start(bf16[256,2048]{1,0:T(8,128)(2,1)} %param.23), channel_id=1, source_target_pairs={{0,2},{2,0},{1,3},{3,1},{4,6},{6,4},{5,7},{7,5},{8,10},{10,8},{9,1... | collective-permute-start | bytes 3145736 | tf_op jit(solution)/shard_map/ppermute | solution.py:233
  208.3 125.0 %collective-permute-start.57 = (bf16[4,1,256,1408]{2,3,1,0:T(8,128)(2,1)}, bf16[4,1,256,1408]{2,3,1,0:T(8,128)(2,1)}, u32[]{:S(2)}, u32[]{:S(2)}) collective-permute-start(bf16[4,1,256,1408]{2,3,1,0:T(8,128)(2,1)} %bitcast.181), channel_id=1, source_target_pairs={{0,4},{4,0},{8,12},{12,8},{16,20},{20,16},{24,28},{28,24},{1,5},{5... | collective-permute-start | bytes 8650760 | tf_op jit(solution)/shard_map/ppermute | solution.py:261
  235.2 44.1 %collective-permute-start.43 = (bf16[2,256,1408]{2,1,0:T(8,128)(2,1)}, bf16[2,256,1408]{2,1,0:T(8,128)(2,1)}, u32[]{:S(2)}, u32[]{:S(2)}) collective-permute-start(bf16[2,256,1408]{2,1,0:T(8,128)(2,1)} %get-tuple-element.63), channel_id=1, source_target_pairs={{0,8},{4,12},{1,9},{5,13},{2,10},{6,14},{3,11},{7,15}} | collective-permute-start | bytes 4325384 | tf_op jit(solution)/shard_map/ppermute | solution.py:283
  241.6 33.7 %collective-permute-start.10 = (bf16[256,2048]{1,0:T(8,128)(2,1)}, bf16[256,2048]{1,0:T(8,128)(2,1)}, u32[]{:S(2)}, u32[]{:S(2)}) collective-permute-start(bf16[256,2048]{1,0:T(8,128)(2,1)} %get-tuple-element.72), channel_id=1, source_target_pairs={{0,2},{2,0},{1,3},{3,1},{4,6},{6,4},{5,7},{7,5},{8,10},{10,8},{9,1... | collective-permute-start | bytes 3145736 | tf_op jit(solution)/shard_map/ppermute | solution.py:233
  272.4 64.5 %collective-permute-start.50 = (bf16[4,1,256,1408]{3,2,1,0:T(8,128)(2,1)S(1)}, bf16[4,1,256,1408]{3,2,1,0:T(8,128)(2,1)S(1)}, u32[]{:S(2)}, u32[]{:S(2)}) collective-permute-start(bf16[4,1,256,1408]{3,2,1,0:T(8,128)(2,1)S(1)} %dynamic-slice_bitcast_fusion), channel_id=1, source_target_pairs={{0,4},{4,0},{8,12},{12,8},{16,20},{20,16},{24,28},{28,24},{1,5},{5... | collective-permute-start | bytes 8650760 | tf_op jit(solution)/shard_map/ppermute | solution.py:261
  279.4 44.1 %collective-permute-start.11 = (bf16[256,2048]{1,0:T(8,128)(2,1)S(1)}, bf16[256,2048]{1,0:T(8,128)(2,1)}, u32[]{:S(2)}, u32[]{:S(2)}) collective-permute-start(bf16[256,2048]{1,0:T(8,128)(2,1)S(1)} %fusion.36), channel_id=1, source_target_pairs={{0,1},{1,0},{2,3},{3,2},{4,5},{5,4},{6,7},{7,6},{8,9},{9,8},{10,11... | collective-permute-start | bytes 3145736 | tf_op jit(solution)/shard_map/ppermute | solution.py:237
  301.3 39.2 %collective-permute-start.46 = (bf16[2,256,1408]{2,1,0:T(8,128)(2,1)}, bf16[2,256,1408]{2,1,0:T(8,128)(2,1)S(1)}, u32[]{:S(2)}, u32[]{:S(2)}) collective-permute-start(bf16[2,256,1408]{2,1,0:T(8,128)(2,1)} %get-tuple-element.64), channel_id=1, source_target_pairs={{24,16},{28,20},{25,17},{29,21},{26,18},{30,22},{27,19},{31,23}} | collective-permute-start | bytes 4325384 | tf_op jit(solution)/shard_map/ppermute | solution.py:284
  304.6 37.5 %collective-permute-start.44 = (bf16[2,256,1408]{2,1,0:T(8,128)(2,1)}, bf16[2,256,1408]{2,1,0:T(8,128)(2,1)S(1)}, u32[]{:S(2)}, u32[]{:S(2)}) collective-permute-start(bf16[2,256,1408]{2,1,0:T(8,128)(2,1)} %bitcast_add_fusion.4), channel_id=1, source_target_pairs={{0,8},{4,12},{8,16},{12,20},{1,9},{5,13},{9,17},{13,21},{2,10},{6,... | collective-permute-start | bytes 4325384 | tf_op jit(solution)/shard_map/ppermute | solution.py:283
  340.5 98.1 %collective-permute-start.61 = (bf16[256,1408]{0,1:T(8,128)(2,1)}, bf16[256,1408]{0,1:T(8,128)(2,1)}, u32[]{:S(2)}, u32[]{:S(2)}) collective-permute-start(bf16[256,1408]{0,1:T(8,128)(2,1)} %get-tuple-element.76), channel_id=1, source_target_pairs={{24,16},{28,20},{25,17},{29,21},{26,18},{30,22},{27,19},{31,23}} | collective-permute-start | bytes 2162696 | tf_op jit(solution)/shard_map/ppermute | solution.py:284
  342.1 27.6 %collective-permute-start.51 = (bf16[256,1408]{1,0:T(8,128)(2,1)S(1)}, bf16[256,1408]{1,0:T(8,128)(2,1)S(1)}, u32[]{:S(2)}, u32[]{:S(2)}) collective-permute-start(bf16[256,1408]{1,0:T(8,128)(2,1)S(1)} %get-tuple-element.79), channel_id=1, source_target_pairs={{0,8},{4,12},{1,9},{5,13},{2,10},{6,14},{3,11},{7,15}} | collective-permute-start | bytes 2162696 | tf_op jit(solution)/shard_map/ppermute | solution.py:283
  354.6 92.9 %collective-permute-start.54 = (bf16[256,1408]{1,0:T(8,128)(2,1)}, bf16[256,1408]{1,0:T(8,128)(2,1)}, u32[]{:S(2)}, u32[]{:S(2)}) collective-permute-start(bf16[256,1408]{1,0:T(8,128)(2,1)} %get-tuple-element.80), channel_id=1, source_target_pairs={{24,16},{28,20},{25,17},{29,21},{26,18},{30,22},{27,19},{31,23}} | collective-permute-start | bytes 2162696 | tf_op jit(solution)/shard_map/ppermute | solution.py:284
  357.8 99.3 %collective-permute-start.47 = (bf16[2,256,1408]{2,1,0:T(8,128)(2,1)}, bf16[2,256,1408]{2,1,0:T(8,128)(2,1)}, u32[]{:S(2)}, u32[]{:S(2)}) collective-permute-start(bf16[2,256,1408]{2,1,0:T(8,128)(2,1)} %get-tuple-element.62), channel_id=1, source_target_pairs={{24,16},{28,20},{16,8},{20,12},{25,17},{29,21},{17,9},{21,13},{26,... | collective-permute-start | bytes 4325384 | tf_op jit(solution)/shard_map/ppermute | solution.py:284
  369.6 74.4 %collective-permute-start.59 = (bf16[256,1408]{0,1:T(8,128)(2,1)}, bf16[256,1408]{0,1:T(8,128)(2,1)}, u32[]{:S(2)}, u32[]{:S(2)}) collective-permute-start(bf16[256,1408]{0,1:T(8,128)(2,1)} %bitcast_add_fusion.10), channel_id=1, source_target_pairs={{0,8},{4,12},{8,16},{12,20},{1,9},{5,13},{9,17},{13,21},{2,10},{6,... | collective-permute-start | bytes 2162696 | tf_op jit(solution)/shard_map/ppermute | solution.py:283
  438.7 96.7 %collective-permute-start.45 = (bf16[2,256,1408]{2,1,0:T(8,128)(2,1)}, bf16[2,256,1408]{2,1,0:T(8,128)(2,1)S(1)}, u32[]{:S(2)}, u32[]{:S(2)}) collective-permute-start(bf16[2,256,1408]{2,1,0:T(8,128)(2,1)} %get-tuple-element.61), channel_id=1, source_target_pairs={{0,8},{4,12},{8,16},{12,20},{16,24},{20,28},{1,9},{5,13},{9,17},{1... | collective-permute-start | bytes 4325384 | tf_op jit(solution)/shard_map/ppermute | solution.py:283
  447.6 51.6 %collective-permute-start.29 = (bf16[4,1,256,640]{2,3,1,0:T(8,128)(2,1)S(1)}, bf16[4,1,256,640]{2,3,1,0:T(8,128)(2,1)S(1)}, u32[]{:S(2)}, u32[]{:S(2)}) collective-permute-start(bf16[4,1,256,640]{2,3,1,0:T(8,128)(2,1)S(1)} %bitcast.184), channel_id=1, source_target_pairs={{0,4},{4,0},{8,12},{12,8},{16,20},{20,16},{24,28},{28,24},{1,5},{5... | collective-permute-start | bytes 3932168 | tf_op jit(solution)/shard_map/ppermute | solution.py:261
  460.3 121.2 %collective-permute-start.21 = (bf16[256,2048]{1,0:T(8,128)(2,1)}, bf16[256,2048]{1,0:T(8,128)(2,1)S(1)}, u32[]{:S(2)}, u32[]{:S(2)}) collective-permute-start(bf16[256,2048]{1,0:T(8,128)(2,1)} %get-tuple-element.67), channel_id=1, source_target_pairs={{0,2},{2,0},{1,3},{3,1},{4,6},{6,4},{5,7},{7,5},{8,10},{10,8},{9,1... | collective-permute-start | bytes 3145736 | tf_op jit(solution)/shard_map/ppermute | solution.py:233
  470.5 66.2 %collective-permute-start.48 = (bf16[2,256,1408]{2,1,0:T(8,128)(2,1)S(1)}, bf16[2,256,1408]{2,1,0:T(8,128)(2,1)S(1)}, u32[]{:S(2)}, u32[]{:S(2)}) collective-permute-start(bf16[2,256,1408]{2,1,0:T(8,128)(2,1)S(1)} %bitcast_add_fusion.3), channel_id=1, source_target_pairs={{24,16},{28,20},{16,8},{20,12},{8,0},{12,4},{25,17},{29,21},{17,9}... | collective-permute-start | bytes 4325384 | tf_op jit(solution)/shard_map/ppermute | solution.py:284
  503.8 36.1 %collective-permute-start.60 = (bf16[256,1408]{0,1:T(8,128)(2,1)S(1)}, bf16[256,1408]{0,1:T(8,128)(2,1)S(1)}, u32[]{:S(2)}, u32[]{:S(2)}) collective-permute-start(bf16[256,1408]{0,1:T(8,128)(2,1)S(1)} %get-tuple-element.73), channel_id=1, source_target_pairs={{0,8},{4,12},{8,16},{12,20},{16,24},{20,28},{1,9},{5,13},{9,17},{1... | collective-permute-start | bytes 2162696 | tf_op jit(solution)/shard_map/ppermute | solution.py:283
  510.3 53.3 %collective-permute-start.53 = (bf16[256,1408]{1,0:T(8,128)(2,1)S(1)}, bf16[256,1408]{1,0:T(8,128)(2,1)S(1)}, u32[]{:S(2)}, u32[]{:S(2)}) collective-permute-start(bf16[256,1408]{1,0:T(8,128)(2,1)S(1)} %get-tuple-element.77), channel_id=1, source_target_pairs={{0,8},{4,12},{8,16},{12,20},{16,24},{20,28},{1,9},{5,13},{9,17},{1... | collective-permute-start | bytes 2162696 | tf_op jit(solution)/shard_map/ppermute | solution.py:283
  536.7 33.2 %collective-permute-start.56 = (bf16[256,1408]{1,0:T(8,128)(2,1)S(1)}, bf16[256,1408]{1,0:T(8,128)(2,1)S(1)}, u32[]{:S(2)}, u32[]{:S(2)}) collective-permute-start(bf16[256,1408]{1,0:T(8,128)(2,1)S(1)} %bitcast_add_fusion.13), channel_id=1, source_target_pairs={{24,16},{28,20},{16,8},{20,12},{8,0},{12,4},{25,17},{29,21},{17,9}... | collective-permute-start | bytes 2162696 | tf_op jit(solution)/shard_map/ppermute | solution.py:284
  540.0 42.4 %collective-permute-start.23 = (bf16[256,2048]{1,0:T(8,128)(2,1)S(1)}, bf16[256,2048]{1,0:T(8,128)(2,1)S(1)}, u32[]{:S(2)}, u32[]{:S(2)}) collective-permute-start(bf16[256,2048]{1,0:T(8,128)(2,1)S(1)} %fusion.31), channel_id=1, source_target_pairs={{0,1},{1,0},{2,3},{3,2},{4,5},{5,4},{6,7},{7,6},{8,9},{9,8},{10,11... | collective-permute-start | bytes 3145736 | tf_op jit(solution)/shard_map/ppermute | solution.py:237
  (91 other events, 1236.4 us)
